TPU v7x, 32 devices: a whole 2x2x4 slice. The times are simulated.
32 devices in a mesh: slab: 4 (over z), inner: 8 (over y, x, core).
Axes of the slice: x: 2, y: 2, z: 4, core: 2. Of those that a mesh axis runs over, the one named last changes fastest.
Arguments:
- coords_fine: float32 [3, 32768], P(None, ('slab', 'inner')), may hold values from 0 to 1, as said below
- coords_coarse: float32 [3, 131072], P(None, 'slab'), may hold values from 0 to 1, as said below
- set_index: int32 [4, 16, 8, 512], P('slab', None, 'inner'), may hold values from 0 to 106495, as said below
- counts: int32 [4, 16, 8], P('slab', None, 'inner'), may hold values from 128 to 512
- morton_slot: int32 [4, 16, 8], P('slab', None, 'inner'), may hold values from 0 to 127, as said below
Outputs:
- factor_blocks: float32 [4, 8, 16, 64, 512], P('slab', 'inner')
Inputs may be any that keep to these rules, and one draw needn't show every extreme that they name: `coords_fine`: x and y lie in [0, 1]; the z of a point of slab b lies in [b / 4, (b + 1) / 4]. `coords_coarse`: x and y lie in [0, 1]; the z of a point of slab b lies in [b / 4, (b + 1) / 4]. `set_index`: every entry names a finest-level point of the supernode's own slab or a coarse-level point of its own slab or of a slab directly beside it (never a slab outside 0 to 4 - 1); the last 64 entries are the supernode's own points, and every finest-level point of a slab is the own point of exactly one of its supernodes. `morton_slot`: in each slab every place occurs once; at most 2 supernodes of one device have places of one owner (place // 16), and this most is reached.
All inputs are finite; a program needn't handle non-finite values.
Results may differ from a plain program's by a relative error of at most 0.0003.
Values sent between devices are 32-bit elements; how exact they have to be, the bound alone decides.
A program may use at most 320 MiB of HBM per device.

v0:
```python
import math

import jax
import jax.numpy as jnp
from jax import lax
from jax.experimental import pallas as pl
from jax.experimental.pallas import tpu as pltpu
from jax.sharding import PartitionSpec as P

MEMB = 64
LENGTH_SCALE = 0.2
NUGGET = 0.5
LANES = 128
F32 = jnp.float32
BF16 = jnp.bfloat16


def split(x):
    high = x.astype(BF16)
    return high, (x - high.astype(F32)).astype(BF16)


def dot(a, b, dims=((1,), (0,))):
    return lax.dot_general(a, b, (dims, ((), ())), preferred_element_type=F32)


def dot3(a, b, dims=((1,), (0,))):
    ah, al = split(a)
    bh, bl = split(b)
    return dot(ah, bh, dims) + (dot(ah, bl, dims) + dot(al, bh, dims))


def gather_points(table_ref, index_ref, pts_ref, nsn, width):
    lane = lax.broadcasted_iota(jnp.int32, (8, LANES), 1)
    chunks = width // LANES

    def chunk(n, _):
        s = n // chunks
        c = n % chunks
        acc = jnp.zeros((8, LANES), F32)
        for p in range(LANES):
            number = index_ref[s, c * LANES + p]
            start = pl.multiple_of((number >> 7) * LANES, LANES)
            tile = table_ref[:, pl.ds(start, LANES)]
            tile = pltpu.roll(tile, (p - number) & (LANES - 1), 1)
            acc = jnp.where(lane == p, tile, acc)
        pts_ref[s, :, pl.ds(pl.multiple_of(c * LANES, LANES), LANES)] = acc
        return 0

    lax.fori_loop(0, nsn * chunks, chunk, 0)


def build_kernels(count_ref, pts_ref, k_ref, nsn, width):
    step = 64

    def one(s, _):
        first = width - count_ref[s]
        rows = pts_ref[s]
        cols = jnp.transpose(rows)
        for r in range(width // step):
            lo = r * step
            base = lo // LANES * LANES
            wide = width - base
            square = None
            for c in range(3):
                diff = cols[lo : lo + step, c : c + 1] - rows[c : c + 1, base:]
                square = diff * diff if square is None else square + diff * diff
            dist = jnp.sqrt(square) * (math.sqrt(3.0) / LENGTH_SCALE)
            kern = (1.0 + dist) * jnp.exp(-dist)
            p = lo + lax.broadcasted_iota(jnp.int32, (step, wide), 0)
            q = base + lax.broadcasted_iota(jnp.int32, (step, wide), 1)
            kern = jnp.where(jnp.minimum(p, q) >= first, kern, 0.0)
            kern = kern + jnp.where(p == q, jnp.where(p >= first, NUGGET, 1.0), 0.0)
            k_ref[s, lo : lo + step, base:] = kern
        return 0

    lax.fori_loop(0, nsn, one, 0)


def leaf(k_ref, work_ref, inv_ref, t, nsn):
    row = lax.broadcasted_iota(jnp.int32, (MEMB, LANES), 0)
    lane = lax.broadcasted_iota(jnp.int32, (MEMB, LANES), 1)
    lane_one = lax.broadcasted_iota(jnp.int32, (1, LANES), 1)
    lo = t * MEMB
    base = lo // LANES * LANES
    eye = (row + MEMB == lane).astype(F32)

    def load(s, _):
        tile = k_ref[s, lo : lo + MEMB, base : base + LANES]
        if lo != base:
            tile = pltpu.roll(tile, MEMB, 1)
        work_ref[s] = jnp.where(lane < MEMB, tile, eye)
        return 0

    lax.fori_loop(0, nsn, load, 0)

    for half in range(2):
        top = half * (MEMB // 2)
        tall = MEMB - top

        def pivot(k, _):
            hit = lane[:tall] == k
            below = row[:tall] + top > k
            for s in range(nsn):
                full = work_ref[s, top:]
                now = work_ref[s, pl.ds(k, 1), :]
                piv = jnp.sum(jnp.where(lane_one == k, now, 0.0), axis=1, keepdims=True)
                col = jnp.sum(jnp.where(hit, full, 0.0), axis=1, keepdims=True)
                work_ref[s, top:] = full - jnp.where(below, col, 0.0) * (now / piv)
            return 0

        lax.fori_loop(top, top + MEMB // 2, pivot, 0)

    def finish(s, _):
        full = work_ref[s]
        diag = jnp.sum(jnp.where(row == lane, full, 0.0), axis=1, keepdims=True)
        inv_ref[t, s] = pltpu.roll(full, MEMB, 1)[:, :MEMB] * lax.rsqrt(diag)
        return 0

    lax.fori_loop(0, nsn, finish, 0)


def update(k_ref, inv_ref, t, nsn, width):
    lo = t * MEMB
    after = lo + MEMB
    base = after // LANES * LANES

    def one(n, _):
        for u in range(2):
            s = n * 2 + u
            rows = dot3(inv_ref[t, s], k_ref[s, lo:after, base:])
            k_ref[s, lo:after, base:] = rows
            high, low = split(rows)
            left = jnp.concatenate([high, low, high], axis=0)
            right = jnp.concatenate([high, high, low], axis=0)
            for r in range(base, width, LANES):
                piece = dot(left[:, r - base : r - base + LANES], right[:, r - base :], ((0,), (0,)))
                k_ref[s, r : r + LANES, r:] = k_ref[s, r : r + LANES, r:] - piece
        return 0

    def one_half(n, _):
        for u in range(2):
            s = n * 2 + u
            rows = dot3(inv_ref[t, s], k_ref[s, lo:after, base:])
            high, low = split(rows)
            left = jnp.concatenate([high, low, high], axis=0)
            right = jnp.concatenate([high, high, low], axis=0)
            for r in range(base, width, LANES):
                piece = dot(left[:, r - base : r - base + LANES], right[:, r - base :], ((0,), (0,)))
                skip = MEMB if r == base else 0
                k_ref[s, r + skip : r + LANES, r:] = k_ref[s, r + skip : r + LANES, r:] - piece[skip:]
            k_ref[s, lo:after, base:] = rows
        return 0

    lax.fori_loop(0, nsn // 2, one if base == after else one_half, 0)


def back(k_ref, inv_ref, target_ref, out_ref, rest_ref, nsn, width):
    stages = width // MEMB

    def one(n, _):
        for u in range(2):
            s = n * 2 + u
            now = jnp.transpose(inv_ref[stages - 1, s])
            rest_ref[u, width - MEMB :] = now
            for j in range(stages - 1, 0, -1):
                lo = j * MEMB
                piece = dot3(k_ref[s, :lo, lo : lo + MEMB], now)
                if j == stages - 1:
                    rest_ref[u, :lo] = -piece
                else:
                    rest_ref[u, :lo] = rest_ref[u, :lo] - piece
                now = dot3(inv_ref[j - 1, s], rest_ref[u, lo - MEMB : lo], ((0,), (0,)))
                rest_ref[u, lo - MEMB : lo] = now
            out_ref[target_ref[s]] = jnp.transpose(rest_ref[u])
        return 0

    lax.fori_loop(0, nsn // 2, one, 0)


def factor_kernel(index_ref, count_ref, target_ref, table_ref, out_ref, pts_ref, k_ref, work_ref, inv_ref, rest_ref):
    nsn, width = index_ref.shape
    stages = width // MEMB
    gather_points(table_ref, index_ref, pts_ref, nsn, width)
    build_kernels(count_ref, pts_ref, k_ref, nsn, width)
    for t in range(stages):
        leaf(k_ref, work_ref, inv_ref, t, nsn)
        if t < stages - 1:
            update(k_ref, inv_ref, t, nsn, width)
    back(k_ref, inv_ref, target_ref, out_ref, rest_ref, nsn, width)


def factor_all(table, wanted, count, target, slots):
    nsn, width = wanted.shape
    smem = pl.BlockSpec(memory_space=pltpu.SMEM)
    vmem = pl.BlockSpec(memory_space=pltpu.VMEM)
    return pl.pallas_call(
        factor_kernel,
        out_shape=jax.ShapeDtypeStruct((slots, MEMB, width), F32),
        in_specs=[smem, smem, smem, vmem],
        out_specs=vmem,
        scratch_shapes=[
            pltpu.VMEM((nsn, 8, width), F32),
            pltpu.VMEM((nsn, width, width), F32),
            pltpu.VMEM((nsn, MEMB, LANES), F32),
            pltpu.VMEM((width // MEMB, nsn, MEMB, MEMB), F32),
            pltpu.VMEM((2, width, MEMB), F32),
        ],
        compiler_params=pltpu.CompilerParams(vmem_limit_bytes=50 * 1024 * 1024),
        name="factor",
    )(wanted, count, target, table)


def place_kernel(spot_ref, got_ref, out_ref, sems):
    nlocal = out_ref.shape[0]
    for i in range(got_ref.shape[0]):
        @pl.when(spot_ref[i] < nlocal)
        def _():
            pltpu.make_async_copy(got_ref.at[i], out_ref.at[spot_ref[i]], sems.at[i]).start()
    for i in range(got_ref.shape[0]):
        @pl.when(spot_ref[i] < nlocal)
        def _():
            pltpu.make_async_copy(got_ref.at[i], out_ref.at[spot_ref[i]], sems.at[i]).wait()


def place_all(got, spot, nlocal):
    return pl.pallas_call(
        place_kernel,
        out_shape=jax.ShapeDtypeStruct((nlocal,) + got.shape[1:], F32),
        in_specs=[pl.BlockSpec(memory_space=pltpu.SMEM), pl.BlockSpec(memory_space=pl.ANY)],
        out_specs=pl.BlockSpec(memory_space=pl.ANY),
        scratch_shapes=[pltpu.SemaphoreType.DMA((got.shape[0],))],
        name="place",
    )(spot, got)


def body(coords_fine, coords_coarse, set_index, counts, morton_slot):
    width = set_index.shape[-1]
    ends = lax.axis_size("slab") - 1
    fine = lax.all_gather(coords_fine, "inner", axis=1, tiled=True)
    below = lax.ppermute(coords_coarse, "slab", [(i, i + 1) for i in range(ends)])
    above = lax.ppermute(coords_coarse, "slab", [(i + 1, i) for i in range(ends)])
    table = jnp.concatenate([fine, below, coords_coarse, above], axis=1)
    table = jnp.pad(table, ((0, 5), (0, 0)))
    wanted = set_index.reshape(-1, width)
    count_here = counts.reshape(-1)
    places = morton_slot.reshape(-1)
    nlocal = wanted.shape[0]
    peers = lax.axis_size("inner")
    capacity = max(1, nlocal // peers)
    slots = peers * capacity
    owner = places // nlocal
    spot = places % nlocal
    order = jnp.arange(nlocal, dtype=jnp.int32)
    earlier = (owner[:, None] == owner[None, :]) & (order[None, :] < order[:, None])
    target = owner * capacity + jnp.sum(earlier.astype(jnp.int32), axis=1)
    hits = target[None, :] == jnp.arange(slots, dtype=jnp.int32)[:, None]
    send_spot = nlocal + jnp.sum(jnp.where(hits, spot[None, :] - nlocal, 0), axis=1)
    got_spot = lax.all_to_all(send_spot, "inner", split_axis=0, concat_axis=0, tiled=True)
    blocks = factor_all(table, wanted, count_here, target, slots)
    got_blocks = lax.all_to_all(blocks, "inner", split_axis=0, concat_axis=0, tiled=True)
    result = place_all(got_blocks, got_spot, nlocal)
    return result.reshape(1, 1, nlocal, MEMB, width)


def solution(mesh):
    placed = (
        P(None, ("slab", "inner")),
        P(None, "slab"),
        P("slab", None, "inner", None),
        P("slab", None, "inner"),
        P("slab", None, "inner"),
    )
    return jax.shard_map(
        body,
        mesh=mesh,
        in_specs=placed,
        out_specs=P("slab", "inner", None, None, None),
        check_vma=False,
    )
```

profile of v0, /device:TPU:0, one launch (start us, length us, event | category | flops | bytes accessed | tf_op | source)
XLA Modules:
  0.0 1001.5 jit_solution(11947053037312281227)
XLA Ops:
  0.0 0.0 copy-start
  0.0 5.1 collective-permute-start
  5.1 1.3 collective-permute-start.1
  6.4 0.7 and_select_fusion.1
  7.1 0.2 convert_reduce_fusion
  7.2 0.1 select_reduce_fusion
  7.4 0.7 add.49
  8.1 3.7 all-to-all-start
  11.8 0.8 copy.10
  12.5 9.9 all_gather.3
  22.4 0.0 collective-permute-done
  22.4 0.0 collective-permute-done.1
  22.4 3.2 select_maximum_fusion.table_ref
  25.6 0.0 copy-done
  25.6 878.9 %factor.1 = f32[16,64,512]{2,1,0:T(8,128)} custom-call(s32[16,512]{1,0:T(8,128)S(1)} %bitcast.22, s32[16]{0:T(128)S(1)} %bitcast.23, s32[16]{0:T(128)S(1)} %multiply_add_fusion.target_ref, f32[8,106496]{1,0:T(8,128)} %select_maximum_fusion.table_ref), custom_call_target="tpu_custom_call" | custom-call | tf_op jit(solution)/shard_map/factor/pallas_call | solution.py:197
  904.5 0.0 all-to-all-done
  904.5 3.6 all-to-all-start.1
  908.1 0.5 broadcast.161
  908.6 0.6 reduce.3
  909.2 0.6 all_to_all.9.spot_ref
  909.8 24.9 %all-to-all-done.1.got_ref = f32[16,64,512]{2,1,0:T(8,128)S(1)} async-done(((f32[16,64,512]{2,1,0:T(8,128)}), f32[16,64,512]{2,1,0:T(8,128)S(1)}, u32[]{:S(2)}, u32[]{:S(2)}) %all-to-all-start.1) | async-done | bytes 2097184 | tf_op jit(solution)/shard_map/all_to_all | solution.py:261
  934.7 0.0 copy-start.1
  934.7 1.3 copy-done.1
  936.1 65.4 %place.1 = f32[16,64,512]{2,1,0:T(8,128)} custom-call(s32[16]{0:T(128)} %all_to_all.9.spot_ref, f32[16,64,512]{2,1,0:T(8,128)} %copy-done.1), custom_call_target="tpu_custom_call" | custom-call | tf_op jit(solution)/shard_map/place/pallas_call | solution.py:227
  (2 shorter events, 0.0 us)
Async XLA Ops:
  0.0 25.6 %copy-start = (s32[1,16,1]{1,2,0:T(1,128)S(1)}, s32[1,16,1]{1,2,0:T(1,128)}, u32[]{:S(2)}) copy-start(s32[1,16,1]{1,2,0:T(1,128)} %param.8) | copy-start | bytes 196
  0.0 22.4 %collective-permute-start = (f32[3,32768]{1,0:T(4,128)}, f32[3,32768]{1,0:T(4,128)S(1)}, u32[]{:S(2)}, u32[]{:S(2)}) collective-permute-start(f32[3,32768]{1,0:T(4,128)} %param.6), channel_id=1, source_target_pairs={{0,8},{8,16},{16,24},{1,9},{9,17},{17,25},{2,10},{10,18},{18,26},{... | collective-permute-start | bytes 1179656 | tf_op jit(solution)/shard_map/ppermute | solution.py:241
  5.1 17.3 %collective-permute-start.1 = (f32[3,32768]{1,0:T(4,128)}, f32[3,32768]{1,0:T(4,128)S(1)}, u32[]{:S(2)}, u32[]{:S(2)}) collective-permute-start(f32[3,32768]{1,0:T(4,128)} %param.6), channel_id=1, source_target_pairs={{8,0},{16,8},{24,16},{9,1},{17,9},{25,17},{10,2},{18,10},{26,18},{... | collective-permute-start | bytes 1179656 | tf_op jit(solution)/shard_map/ppermute | solution.py:242
  8.1 896.5 %all-to-all-start = ((s32[8,2,1]{1,2,0:T(1,128)}), s32[8,2,1]{1,2,0:T(1,128)S(1)}, u32[]{:S(2)}, u32[]{:S(2)}) async-start(s32[8,2,1]{1,2,0:T(1,128)} %bitcast.1), calls=%async_computation | async-start | bytes 8192 | tf_op jit(solution)/shard_map/all_to_all | solution.py:259
  904.5 30.2 %all-to-all-start.1 = ((f32[16,64,512]{2,1,0:T(8,128)}), f32[16,64,512]{2,1,0:T(8,128)S(1)}, u32[]{:S(2)}, u32[]{:S(2)}) async-start(f32[16,64,512]{2,1,0:T(8,128)} %factor.1), calls=%async_computation.1 | async-start | bytes 4194304 | tf_op jit(solution)/shard_map/all_to_all | solution.py:261
  934.7 1.3 copy-start.1
where the time goes:
time: 1000 us
  Pallas kernels  944 us (94%)
  waiting for transfers between devices  24.9 us (2%)
  starting transfers between devices  13.7 us (1%)
    pallas_call x1, Pallas kernels, factor_all(): pl.pallas_call(factor_kernel, out_shape=jax.ShapeDtypeStruct((slots, MEMB...  879 us
    pallas_call x1, Pallas kernels, place_all(): pl.pallas_call(place_kernel, out_shape=jax.ShapeDtypeStruct((nlocal,) + g...  65.4 us
    all_to_all x1, waiting for transfers between devices, body(): lax.all_to_all(blocks, 'inner', split_axis=0, concat_axis=0, tiled=True)  24.9 us
  transfers between devices with their start and end apart: 4, of which 1 were waited for; matrix products, arithmetic and copies ran while one was open for 1% of the time, Pallas kernels for 88%

commit v1 on v0

--- a/solution.py
+++ b/solution.py
@@ -101,12 +101,13 @@
         def pivot(k, _):
             hit = lane[:tall] == k
             below = row[:tall] + top > k
+            nows = [work_ref[s, pl.ds(k, 1), :] for s in range(nsn)]
+            pivs = [jnp.sum(jnp.where(lane_one == k, now, 0.0), axis=1, keepdims=True) for now in nows]
+            nows = [now / piv for now, piv in zip(nows, pivs)]
             for s in range(nsn):
                 full = work_ref[s, top:]
-                now = work_ref[s, pl.ds(k, 1), :]
-                piv = jnp.sum(jnp.where(lane_one == k, now, 0.0), axis=1, keepdims=True)
                 col = jnp.sum(jnp.where(hit, full, 0.0), axis=1, keepdims=True)
-                work_ref[s, top:] = full - jnp.where(below, col, 0.0) * (now / piv)
+                work_ref[s, top:] = full - jnp.where(below, col, 0.0) * nows[s]
             return 0
 
         lax.fori_loop(top, top + MEMB // 2, pivot, 0)
@@ -125,57 +126,56 @@
     after = lo + MEMB
     base = after // LANES * LANES
 
-    def one(n, _):
-        for u in range(2):
-            s = n * 2 + u
-            rows = dot3(inv_ref[t, s], k_ref[s, lo:after, base:])
-            k_ref[s, lo:after, base:] = rows
-            high, low = split(rows)
-            left = jnp.concatenate([high, low, high], axis=0)
-            right = jnp.concatenate([high, high, low], axis=0)
-            for r in range(base, width, LANES):
-                piece = dot(left[:, r - base : r - base + LANES], right[:, r - base :], ((0,), (0,)))
-                k_ref[s, r : r + LANES, r:] = k_ref[s, r : r + LANES, r:] - piece
-        return 0
-
-    def one_half(n, _):
-        for u in range(2):
-            s = n * 2 + u
-            rows = dot3(inv_ref[t, s], k_ref[s, lo:after, base:])
-            high, low = split(rows)
-            left = jnp.concatenate([high, low, high], axis=0)
-            right = jnp.concatenate([high, high, low], axis=0)
-            for r in range(base, width, LANES):
-                piece = dot(left[:, r - base : r - base + LANES], right[:, r - base :], ((0,), (0,)))
-                skip = MEMB if r == base else 0
-                k_ref[s, r + skip : r + LANES, r:] = k_ref[s, r + skip : r + LANES, r:] - piece[skip:]
-            k_ref[s, lo:after, base:] = rows
-        return 0
-
-    lax.fori_loop(0, nsn // 2, one if base == after else one_half, 0)
+    group = 4
+
+    def some(n, _):
+        sets = [n * group + u for u in range(group)]
+        rows = [dot3(inv_ref[t, s], k_ref[s, lo:after, base:]) for s in sets]
+        parts = [split(x) for x in rows]
+        left = [jnp.concatenate([high, low, high], axis=0) for high, low in parts]
+        right = [jnp.concatenate([high, high, low], axis=0) for high, low in parts]
+        for r in range(base, width, LANES):
+            skip = MEMB if r == base and base != after else 0
+            pieces = [
+                dot(x[:, r - base : r - base + LANES], y[:, r - base :], ((0,), (0,)))[skip:]
+                for x, y in zip(left, right)
+            ]
+            fresh = [k_ref[s, r + skip : r + LANES, r:] - piece for s, piece in zip(sets, pieces)]
+            for s, value in zip(sets, fresh):
+                k_ref[s, r + skip : r + LANES, r:] = value
+        for s, value in zip(sets, rows):
+            k_ref[s, lo:after, base:] = value
+        return 0
+
+    lax.fori_loop(0, nsn // group, some, 0)
 
 
 def back(k_ref, inv_ref, target_ref, out_ref, rest_ref, nsn, width):
     stages = width // MEMB
 
-    def one(n, _):
-        for u in range(2):
-            s = n * 2 + u
-            now = jnp.transpose(inv_ref[stages - 1, s])
-            rest_ref[u, width - MEMB :] = now
-            for j in range(stages - 1, 0, -1):
-                lo = j * MEMB
-                piece = dot3(k_ref[s, :lo, lo : lo + MEMB], now)
+    group = 4
+
+    def some(n, _):
+        sets = [n * group + u for u in range(group)]
+        nows = [jnp.transpose(inv_ref[stages - 1, s]) for s in sets]
+        for u in range(group):
+            rest_ref[u, width - MEMB :] = nows[u]
+        for j in range(stages - 1, 0, -1):
+            lo = j * MEMB
+            pieces = [dot3(k_ref[s, :lo, lo : lo + MEMB], now) for s, now in zip(sets, nows)]
+            for u in range(group):
                 if j == stages - 1:
-                    rest_ref[u, :lo] = -piece
+                    rest_ref[u, :lo] = -pieces[u]
                 else:
-                    rest_ref[u, :lo] = rest_ref[u, :lo] - piece
-                now = dot3(inv_ref[j - 1, s], rest_ref[u, lo - MEMB : lo], ((0,), (0,)))
-                rest_ref[u, lo - MEMB : lo] = now
+                    rest_ref[u, :lo] = rest_ref[u, :lo] - pieces[u]
+            nows = [dot3(inv_ref[j - 1, s], rest_ref[u, lo - MEMB : lo], ((0,), (0,))) for u, s in enumerate(sets)]
+            for u in range(group):
+                rest_ref[u, lo - MEMB : lo] = nows[u]
+        for u, s in enumerate(sets):
             out_ref[target_ref[s]] = jnp.transpose(rest_ref[u])
         return 0
 
-    lax.fori_loop(0, nsn // 2, one, 0)
+    lax.fori_loop(0, nsn // group, some, 0)
 
 
 def factor_kernel(index_ref, count_ref, target_ref, table_ref, out_ref, pts_ref, k_ref, work_ref, inv_ref, rest_ref):
@@ -204,32 +204,29 @@
             pltpu.VMEM((nsn, width, width), F32),
             pltpu.VMEM((nsn, MEMB, LANES), F32),
             pltpu.VMEM((width // MEMB, nsn, MEMB, MEMB), F32),
-            pltpu.VMEM((2, width, MEMB), F32),
+            pltpu.VMEM((4, width, MEMB), F32),
         ],
         compiler_params=pltpu.CompilerParams(vmem_limit_bytes=50 * 1024 * 1024),
         name="factor",
     )(wanted, count, target, table)
 
 
-def place_kernel(spot_ref, got_ref, out_ref, sems):
+def place_kernel(spot_ref, got_ref, out_ref):
     nlocal = out_ref.shape[0]
     for i in range(got_ref.shape[0]):
         @pl.when(spot_ref[i] < nlocal)
         def _():
-            pltpu.make_async_copy(got_ref.at[i], out_ref.at[spot_ref[i]], sems.at[i]).start()
-    for i in range(got_ref.shape[0]):
-        @pl.when(spot_ref[i] < nlocal)
-        def _():
-            pltpu.make_async_copy(got_ref.at[i], out_ref.at[spot_ref[i]], sems.at[i]).wait()
+            out_ref[spot_ref[i]] = got_ref[i]
 
 
 def place_all(got, spot, nlocal):
+    vmem = pl.BlockSpec(memory_space=pltpu.VMEM)
     return pl.pallas_call(
         place_kernel,
         out_shape=jax.ShapeDtypeStruct((nlocal,) + got.shape[1:], F32),
-        in_specs=[pl.BlockSpec(memory_space=pltpu.SMEM), pl.BlockSpec(memory_space=pl.ANY)],
-        out_specs=pl.BlockSpec(memory_space=pl.ANY),
-        scratch_shapes=[pltpu.SemaphoreType.DMA((got.shape[0],))],
+        in_specs=[pl.BlockSpec(memory_space=pltpu.SMEM), vmem],
+        out_specs=vmem,
+        compiler_params=pltpu.CompilerParams(vmem_limit_bytes=16 * 1024 * 1024),
         name="place",
     )(spot, got)
 

time: 1000 us -> 261 us (0.26)
  Pallas kernels: 944 us -> 205 us
    pallas_call x1, Pallas kernels: 879 us -> 203 us  [factor_all(): pl.pallas_call(factor_kernel, out_shape=jax.ShapeDtypeStruct((slots, MEMB...]
    pallas_call x1, Pallas kernels: 65.4 us -> 2.13 us  [place_all(): pl.pallas_call(place_kernel, out_shape=jax.ShapeDtypeStruct((nlocal,) + g...]
  transfers between devices with their start and end apart: 4 -> 4, of which waited for: 1 -> 1; matrix products, arithmetic and copies ran while one was open for 1% -> 3% of each run, Pallas kernels for 88% -> 78%
where the time goes in v1:
time: 261 us
  Pallas kernels  205 us (79%)
  waiting for transfers between devices  25.2 us (10%)
  starting transfers between devices  13.7 us (5%)
  blocking collectives  9.86 us (4%)
  other arithmetic  4.91 us (2%)
    pallas_call x1, Pallas kernels, factor_all(): pl.pallas_call(factor_kernel, out_shape=jax.ShapeDtypeStruct((slots, MEMB...  203 us
    all_to_all x1, waiting for transfers between devices, body(): lax.all_to_all(blocks, 'inner', split_axis=0, concat_axis=0, tiled=True)  25.2 us
    all_gather x1, blocking collectives, body(): fine = lax.all_gather(coords_fine, 'inner', axis=1, tiled=True)  9.86 us
  transfers between devices with their start and end apart: 4, of which 1 were waited for; matrix products, arithmetic and copies ran while one was open for 3% of the time, Pallas kernels for 78%

profile of v1, /device:TPU:0, one launch (start us, length us, event | category | flops | bytes accessed | tf_op | source)
XLA Modules:
  0.0 260.7 jit_solution(14848287322659240600)
XLA Ops:
  0.0 0.0 copy-start
  0.0 5.1 %collective-permute-start = (f32[3,32768]{1,0:T(4,128)}, f32[3,32768]{1,0:T(4,128)S(1)}, u32[]{:S(2)}, u32[]{:S(2)}) collective-permute-start(f32[3,32768]{1,0:T(4,128)} %param.6), channel_id=1, source_target_pairs={{0,8},{8,16},{16,24},{1,9},{9,17},{17,25},{2,10},{10,18},{18,26},{... | collective-permute-start | bytes 1179656 | tf_op jit(solution)/shard_map/ppermute | solution.py:238
  5.1 1.3 collective-permute-start.1
  6.4 0.7 and_select_fusion.1
  7.1 0.2 convert_reduce_fusion
  7.2 0.1 select_reduce_fusion
  7.4 0.7 add.49
  8.1 3.7 %all-to-all-start = ((s32[8,2,1]{1,2,0:T(1,128)}), s32[8,2,1]{1,2,0:T(1,128)S(1)}, u32[]{:S(2)}, u32[]{:S(2)}) async-start(s32[8,2,1]{1,2,0:T(1,128)} %bitcast.1), calls=%async_computation | async-start | bytes 8192 | tf_op jit(solution)/shard_map/all_to_all | solution.py:256
  11.8 0.8 copy.10
  12.5 9.9 %all_gather.3 = f32[3,8192]{1,0:T(4,128)S(1)} all-gather(f32[3,1024]{1,0:T(4,128)} %param.5), channel_id=1, replica_groups=mesh['slab'=4,'inner'=8] {'inner'}, dimensions={1}, use_global_device_ids=true | all-gather | bytes 110592 | tf_op jit(solution)/shard_map/all_gather | solution.py:237
  22.4 0.0 collective-permute-done
  22.4 0.0 collective-permute-done.1
  22.4 3.2 %select_maximum_fusion.table_ref = f32[8,106496]{1,0:T(8,128)} fusion(f32[3,32768]{1,0:T(4,128)S(1)} %collective-permute-done.1, f32[3,32768]{1,0:T(4,128)} %param.6, f32[3,32768]{1,0:T(4,128)S(1)} %collective-permute-done, f32[3,8192]{1,0:T(4,128)S(1)} %all_gather.3), kind=kLoop, calls=%fused_computation | loop fusion | flops 6815744 | bytes 4685824 | tf_op jit(solution)/shard_map/concatenate | solution.py:240
  25.6 0.0 copy-done
  25.6 202.8 %factor.1 = f32[16,64,512]{2,1,0:T(8,128)} custom-call(s32[16,512]{1,0:T(8,128)S(1)} %bitcast.22, s32[16]{0:T(128)S(1)} %bitcast.23, s32[16]{0:T(128)S(1)} %multiply_add_fusion.target_ref, f32[8,106496]{1,0:T(8,128)} %select_maximum_fusion.table_ref), custom_call_target="tpu_custom_call" | custom-call | tf_op jit(solution)/shard_map/factor/pallas_call | solution.py:197
  228.4 0.0 all-to-all-done
  228.4 3.6 %all-to-all-start.1 = ((f32[16,64,512]{2,1,0:T(8,128)}), f32[16,64,512]{2,1,0:T(8,128)S(1)}, u32[]{:S(2)}, u32[]{:S(2)}) async-start(f32[16,64,512]{2,1,0:T(8,128)} %factor.1), calls=%async_computation.1 | async-start | bytes 4194304 | tf_op jit(solution)/shard_map/all_to_all | solution.py:258
  232.0 0.6 broadcast.161
  232.6 0.7 reduce.3
  233.3 0.1 all_to_all.9.spot_ref
  233.4 25.2 %all-to-all-done.1.got_ref = f32[16,64,512]{2,1,0:T(8,128)S(1)} async-done(((f32[16,64,512]{2,1,0:T(8,128)}), f32[16,64,512]{2,1,0:T(8,128)S(1)}, u32[]{:S(2)}, u32[]{:S(2)}) %all-to-all-start.1) | async-done | bytes 2097184 | tf_op jit(solution)/shard_map/all_to_all | solution.py:258
  258.6 2.1 place.1
  (2 shorter events, 0.0 us)
Async XLA Ops:
  0.0 25.6 %copy-start = (s32[1,16,1]{1,2,0:T(1,128)S(1)}, s32[1,16,1]{1,2,0:T(1,128)}, u32[]{:S(2)}) copy-start(s32[1,16,1]{1,2,0:T(1,128)} %param.8) | copy-start | bytes 196
  0.0 22.4 %collective-permute-start = (f32[3,32768]{1,0:T(4,128)}, f32[3,32768]{1,0:T(4,128)S(1)}, u32[]{:S(2)}, u32[]{:S(2)}) collective-permute-start(f32[3,32768]{1,0:T(4,128)} %param.6), channel_id=1, source_target_pairs={{0,8},{8,16},{16,24},{1,9},{9,17},{17,25},{2,10},{10,18},{18,26},{... | collective-permute-start | bytes 1179656 | tf_op jit(solution)/shard_map/ppermute | solution.py:238
  5.1 17.3 %collective-permute-start.1 = (f32[3,32768]{1,0:T(4,128)}, f32[3,32768]{1,0:T(4,128)S(1)}, u32[]{:S(2)}, u32[]{:S(2)}) collective-permute-start(f32[3,32768]{1,0:T(4,128)} %param.6), channel_id=1, source_target_pairs={{8,0},{16,8},{24,16},{9,1},{17,9},{25,17},{10,2},{18,10},{26,18},{... | collective-permute-start | bytes 1179656 | tf_op jit(solution)/shard_map/ppermute | solution.py:239
  8.1 220.3 %all-to-all-start = ((s32[8,2,1]{1,2,0:T(1,128)}), s32[8,2,1]{1,2,0:T(1,128)S(1)}, u32[]{:S(2)}, u32[]{:S(2)}) async-start(s32[8,2,1]{1,2,0:T(1,128)} %bitcast.1), calls=%async_computation | async-start | bytes 8192 | tf_op jit(solution)/shard_map/all_to_all | solution.py:256
  228.4 30.2 %all-to-all-start.1 = ((f32[16,64,512]{2,1,0:T(8,128)}), f32[16,64,512]{2,1,0:T(8,128)S(1)}, u32[]{:S(2)}, u32[]{:S(2)}) async-start(f32[16,64,512]{2,1,0:T(8,128)} %factor.1), calls=%async_computation.1 | async-start | bytes 4194304 | tf_op jit(solution)/shard_map/all_to_all | solution.py:258

commit v2 on v1

--- a/solution.py
+++ b/solution.py
@@ -94,8 +94,8 @@
 
     lax.fori_loop(0, nsn, load, 0)
 
-    for half in range(2):
-        top = half * (MEMB // 2)
+    for part in range(4):
+        top = part * (MEMB // 4)
         tall = MEMB - top
 
         def pivot(k, _):
@@ -110,7 +110,7 @@
                 work_ref[s, top:] = full - jnp.where(below, col, 0.0) * nows[s]
             return 0
 
-        lax.fori_loop(top, top + MEMB // 2, pivot, 0)
+        lax.fori_loop(top, top + MEMB // 4, pivot, 0)
 
     def finish(s, _):
         full = work_ref[s]

time: 261 us -> 253 us (0.969)
  Pallas kernels: 205 us -> 196 us
    pallas_call x1, Pallas kernels: 203 us -> 194 us  [factor_all(): pl.pallas_call(factor_kernel, out_shape=jax.ShapeDtypeStruct((slots, MEMB...]
  transfers between devices with their start and end apart: 4 -> 4, of which waited for: 1 -> 1; matrix products, arithmetic and copies ran while one was open for 3% -> 3% of each run, Pallas kernels for 78% -> 77%
where the time goes in v2:
time: 253 us; the launch traced here: 252 us
  Pallas kernels  196 us (77%)
  waiting for transfers between devices  25.2 us (10%)
  starting transfers between devices  13.7 us (5%)
  blocking collectives  9.86 us (4%)
  other arithmetic  4.91 us (2%)
    pallas_call x1, Pallas kernels, factor_all(): pl.pallas_call(factor_kernel, out_shape=jax.ShapeDtypeStruct((slots, MEMB...  194 us
    all_to_all x1, waiting for transfers between devices, body(): lax.all_to_all(blocks, 'inner', split_axis=0, concat_axis=0, tiled=True)  25.2 us
    all_gather x1, blocking collectives, body(): fine = lax.all_gather(coords_fine, 'inner', axis=1, tiled=True)  9.86 us
    ppermute x1, starting transfers between devices, body(): lax.ppermute(coords_coarse, 'slab', [(i, i + 1) for i in range(ends)])  5.08 us
  transfers between devices with their start and end apart: 4, of which 1 were waited for; matrix products, arithmetic and copies ran while one was open for 3% of the time, Pallas kernels for 77%

profile of v2, /device:TPU:0, one launch (start us, length us, event | category | flops | bytes accessed | tf_op | source)
XLA Modules:
  0.0 252.3 jit_solution(14319177799329285887)
XLA Ops:
  0.0 0.0 copy-start
  0.0 5.1 %collective-permute-start = (f32[3,32768]{1,0:T(4,128)}, f32[3,32768]{1,0:T(4,128)S(1)}, u32[]{:S(2)}, u32[]{:S(2)}) collective-permute-start(f32[3,32768]{1,0:T(4,128)} %param.6), channel_id=1, source_target_pairs={{0,8},{8,16},{16,24},{1,9},{9,17},{17,25},{2,10},{10,18},{18,26},{... | collective-permute-start | bytes 1179656 | tf_op jit(solution)/shard_map/ppermute | solution.py:238
  5.1 1.3 collective-permute-start.1
  6.4 0.7 and_select_fusion.1
  7.1 0.2 convert_reduce_fusion
  7.2 0.1 select_reduce_fusion
  7.4 0.7 add.49
  8.1 3.7 %all-to-all-start = ((s32[8,2,1]{1,2,0:T(1,128)}), s32[8,2,1]{1,2,0:T(1,128)S(1)}, u32[]{:S(2)}, u32[]{:S(2)}) async-start(s32[8,2,1]{1,2,0:T(1,128)} %bitcast.1), calls=%async_computation | async-start | bytes 8192 | tf_op jit(solution)/shard_map/all_to_all | solution.py:256
  11.8 0.8 copy.10
  12.5 9.9 %all_gather.3 = f32[3,8192]{1,0:T(4,128)S(1)} all-gather(f32[3,1024]{1,0:T(4,128)} %param.5), channel_id=1, replica_groups=mesh['slab'=4,'inner'=8] {'inner'}, dimensions={1}, use_global_device_ids=true | all-gather | bytes 110592 | tf_op jit(solution)/shard_map/all_gather | solution.py:237
  22.4 0.0 collective-permute-done
  22.4 0.0 collective-permute-done.1
  22.4 3.2 %select_maximum_fusion.table_ref = f32[8,106496]{1,0:T(8,128)} fusion(f32[3,32768]{1,0:T(4,128)S(1)} %collective-permute-done.1, f32[3,32768]{1,0:T(4,128)} %param.6, f32[3,32768]{1,0:T(4,128)S(1)} %collective-permute-done, f32[3,8192]{1,0:T(4,128)S(1)} %all_gather.3), kind=kLoop, calls=%fused_computation | loop fusion | flops 6815744 | bytes 4685824 | tf_op jit(solution)/shard_map/concatenate | solution.py:240
  25.6 0.0 copy-done
  25.6 194.3 %factor.1 = f32[16,64,512]{2,1,0:T(8,128)} custom-call(s32[16,512]{1,0:T(8,128)S(1)} %bitcast.22, s32[16]{0:T(128)S(1)} %bitcast.23, s32[16]{0:T(128)S(1)} %multiply_add_fusion.target_ref, f32[8,106496]{1,0:T(8,128)} %select_maximum_fusion.table_ref), custom_call_target="tpu_custom_call" | custom-call | tf_op jit(solution)/shard_map/factor/pallas_call | solution.py:197
  219.9 0.0 all-to-all-done
  219.9 3.6 %all-to-all-start.1 = ((f32[16,64,512]{2,1,0:T(8,128)}), f32[16,64,512]{2,1,0:T(8,128)S(1)}, u32[]{:S(2)}, u32[]{:S(2)}) async-start(f32[16,64,512]{2,1,0:T(8,128)} %factor.1), calls=%async_computation.1 | async-start | bytes 4194304 | tf_op jit(solution)/shard_map/all_to_all | solution.py:258
  223.5 0.6 broadcast.161
  224.1 0.7 reduce.3
  224.9 0.1 all_to_all.9.spot_ref
  224.9 25.2 %all-to-all-done.1.got_ref = f32[16,64,512]{2,1,0:T(8,128)S(1)} async-done(((f32[16,64,512]{2,1,0:T(8,128)}), f32[16,64,512]{2,1,0:T(8,128)S(1)}, u32[]{:S(2)}, u32[]{:S(2)}) %all-to-all-start.1) | async-done | bytes 2097184 | tf_op jit(solution)/shard_map/all_to_all | solution.py:258
  250.1 2.1 place.1
  (2 shorter events, 0.0 us)
Async XLA Ops:
  0.0 25.6 %copy-start = (s32[1,16,1]{1,2,0:T(1,128)S(1)}, s32[1,16,1]{1,2,0:T(1,128)}, u32[]{:S(2)}) copy-start(s32[1,16,1]{1,2,0:T(1,128)} %param.8) | copy-start | bytes 196
  0.0 22.4 %collective-permute-start = (f32[3,32768]{1,0:T(4,128)}, f32[3,32768]{1,0:T(4,128)S(1)}, u32[]{:S(2)}, u32[]{:S(2)}) collective-permute-start(f32[3,32768]{1,0:T(4,128)} %param.6), channel_id=1, source_target_pairs={{0,8},{8,16},{16,24},{1,9},{9,17},{17,25},{2,10},{10,18},{18,26},{... | collective-permute-start | bytes 1179656 | tf_op jit(solution)/shard_map/ppermute | solution.py:238
  5.1 17.3 %collective-permute-start.1 = (f32[3,32768]{1,0:T(4,128)}, f32[3,32768]{1,0:T(4,128)S(1)}, u32[]{:S(2)}, u32[]{:S(2)}) collective-permute-start(f32[3,32768]{1,0:T(4,128)} %param.6), channel_id=1, source_target_pairs={{8,0},{16,8},{24,16},{9,1},{17,9},{25,17},{10,2},{18,10},{26,18},{... | collective-permute-start | bytes 1179656 | tf_op jit(solution)/shard_map/ppermute | solution.py:239
  8.1 211.9 %all-to-all-start = ((s32[8,2,1]{1,2,0:T(1,128)}), s32[8,2,1]{1,2,0:T(1,128)S(1)}, u32[]{:S(2)}, u32[]{:S(2)}) async-start(s32[8,2,1]{1,2,0:T(1,128)} %bitcast.1), calls=%async_computation | async-start | bytes 8192 | tf_op jit(solution)/shard_map/all_to_all | solution.py:256
  219.9 30.2 %all-to-all-start.1 = ((f32[16,64,512]{2,1,0:T(8,128)}), f32[16,64,512]{2,1,0:T(8,128)S(1)}, u32[]{:S(2)}, u32[]{:S(2)}) async-start(f32[16,64,512]{2,1,0:T(8,128)} %factor.1), calls=%async_computation.1 | async-start | bytes 4194304 | tf_op jit(solution)/shard_map/all_to_all | solution.py:258
